TPU v7x, 128 devices: a whole 4x4x4 slice. The times are simulated.
128 devices in a mesh: section: 4 (over x), dom: 32 (over y, z, core).
Axes of the slice: x: 4, y: 4, z: 4, core: 2. Of those that a mesh axis runs over, the one named last changes fastest.
Arguments:
- h0: bfloat16 [2, 49152, 512], P(None, 'dom'), may hold values from -6 to 6
- layer_weight: bfloat16 [8, 512, 512], P('section'), may hold values from -0.25 to 0.25
- tile_vals: bfloat16 [2, 384, 4, 128, 128], P(None, 'dom'), may hold values from -0.375 to 0.375
- tile_cols: int32 [2, 384, 4], P(None, 'dom'), may hold values from 0 to 13, as said below
- boundary: int32 [2, 1024], P(None, 'dom'), may hold values from 0 to 1535
- send_pos: int32 [2, 1024, 8], P(None, 'dom'), may hold values from 0 to 31
- send_count: int32 [2, 1024], P(None, 'dom'), may hold values from 0 to 8, as said below
Outputs:
- section_out: bfloat16 [4, 2, 49152, 512], P('section', None, 'dom')
Inputs may be any that keep to these rules, and one draw needn't show every extreme that they name: `tile_cols`: each partition's row of tiles names its own diagonal tile first; tiles 12 and up are the received rows. `send_count`: zero from a partition to itself; in every batch each partition p sends 8 live slots to partition p + 1 (mod 32).
All inputs are finite; a program needn't handle non-finite values.
Results may differ from a plain program's by a relative error of at most 0.014.
Values may be sent and summed in bfloat16 or wider, within the bound.
No kernel may reach another device: no remote copies, remote signals or barrier semaphores. Data moves between devices by JAX's collectives and lax.ppermute only.
A program may use at most 128 MiB of HBM per device.

v0:
```python
import jax
import jax.numpy as jnp
from jax import lax
from jax.sharding import PartitionSpec as P

restart_share = 0.1
decay_scale = 1.0


def passed_along(x, axis, by):
    devices = lax.axis_size(axis)
    pairs = [(i, i + by) for i in range(devices) if 0 <= i + by < devices]
    return lax.ppermute(x, axis, pairs)


def halo_rows(features, bound_idx, positions, counts):
    picked = features[bound_idx]
    live = jnp.arange(positions.shape[1], dtype=jnp.int32)[None, :] < counts[:, None]
    everyone = lax.all_gather(picked, "dom", axis=0, tiled=True)
    everyone = everyone.reshape(positions.shape[0], -1, picked.shape[1])
    chosen = jnp.take_along_axis(everyone, positions[:, :, None], axis=1)
    return jnp.where(live[:, :, None], chosen, jnp.zeros_like(chosen))


def mix_layer(features, starting, weight, layer_beta, tile_block, column_ids, received):
    width = features.shape[1]
    tile_size = tile_block.shape[-1]
    extra = received.reshape(-1, width)
    spare = -extra.shape[0] % tile_size
    table = jnp.concatenate([features, extra, jnp.zeros((spare, width), features.dtype)], 0)
    table = table.reshape(-1, tile_size, width)
    blocks = table[column_ids]
    mixed = jnp.einsum("rkij,rkjd->rid", tile_block, blocks, preferred_element_type=jnp.float32)
    mixed = mixed.reshape(features.shape)
    zvalue = (1.0 - restart_share) * mixed + restart_share * starting.astype(jnp.float32)
    zround = zvalue.astype(jnp.bfloat16)
    product = jnp.dot(zround, weight, preferred_element_type=jnp.float32)
    return jax.nn.relu((1.0 - layer_beta) * zvalue + layer_beta * product).astype(jnp.bfloat16)


def body(h0, layer_weight, tile_vals, tile_cols, boundary, send_pos, send_count):
    section_pos = lax.axis_index("section")
    section_count = lax.axis_size("section")
    batch_count = h0.shape[0]
    depth = layer_weight.shape[0]
    positions_all, counts_all = (
        lax.all_to_all(send_pos, "dom", split_axis=1, concat_axis=1, tiled=True),
        lax.all_to_all(send_count, "dom", split_axis=1, concat_axis=1, tiled=True),
    )
    results = jnp.zeros(h0.shape, h0.dtype)
    turns = section_count + batch_count - 1
    incoming = jnp.zeros(h0.shape[1:], h0.dtype)
    for turn in range(turns):
        offset = turn - section_pos
        active = (offset >= 0) & (offset < batch_count)
        batch_idx = jnp.clip(offset, 0, batch_count - 1)
        features = incoming
        starting = lax.dynamic_index_in_dim(h0, batch_idx, 0, keepdims=False)
        tile_block = lax.dynamic_index_in_dim(tile_vals, batch_idx, 0, keepdims=False)
        column_ids = lax.dynamic_index_in_dim(tile_cols, batch_idx, 0, keepdims=False)
        bound_idx = lax.dynamic_index_in_dim(boundary, batch_idx, 0, keepdims=False)
        positions = lax.dynamic_index_in_dim(positions_all, batch_idx, 0, keepdims=False)
        counts = lax.dynamic_index_in_dim(counts_all, batch_idx, 0, keepdims=False)
        features = jnp.where(section_pos == 0, starting, features)
        for inner in range(depth):
            layer_no = (section_pos * depth + inner + 1).astype(jnp.float32)
            layer_beta = jnp.log(decay_scale / layer_no + 1.0)
            received = halo_rows(features, bound_idx, positions, counts)
            features = mix_layer(
                features,
                starting,
                layer_weight[inner],
                layer_beta,
                tile_block,
                column_ids,
                received,
            )
        results = jnp.where(
            active, lax.dynamic_update_index_in_dim(results, features, batch_idx, 0), results
        )
        if turn + 1 < turns:
            incoming = passed_along(features, "section", 1)
    return results[None]


def solution(mesh):
    placed = (
        P(None, "dom", None),
        P("section", None, None),
        P(None, "dom", None, None, None),
        P(None, "dom", None),
        P(None, "dom"),
        P(None, "dom", None),
        P(None, "dom"),
    )
    return jax.shard_map(
        body, mesh=mesh, in_specs=placed, out_specs=P("section", None, "dom", None), check_vma=False
    )
```

profile of v0, /device:TPU:15, one launch (start us, length us, event | category | flops | bytes accessed | tf_op | source)
XLA Modules:
  0.0 843.4 jit_solution(282364646544066641)
XLA Ops:
  13.8 8.9 %all-to-all-start = ((s32[2,32,1]{0,2,1:T(1,128)}), s32[2,32,1]{0,2,1:T(1,128)S(1)}, u32[]{:S(2)}, u32[]{:S(2)}) async-start(s32[2,32,1]{0,2,1:T(1,128)} %copy.85), calls=%async_computation | async-start | bytes 32768 | tf_op jit(solution)/shard_map/all_to_all | solution.py:48
  23.6 9.6 %convert_multiply_fusion = (f32[1,1536,512]{2,1,0:T(8,128)}, f32[1,1536,512]{2,1,0:T(8,128)}, f32[1,1536,512]{2,1,0:T(8,128)}, f32[1,1536,512]{2,1,0:T(8,128)}, f32[1,1536,512]{2,1,0:T(8,128)}) fusion(bf16[2,1536,512]{2,1,0:T(8,128)(2,1)} %param.9, s32[]{:T(128)S(6)} %min.20, s32[]{:T(128)S(6)} %min.17, s32[]{:T(128)S(6)} %min.18, s32[]{:T(128)S(6)} %min.19, ...), kind=kLoop, calls=%fused_computation.92 | loop fusion | flops 7864320 | bytes 23592980 | tf_op jit(solution)/shard_map/mul | solution.py:35
  33.4 7.4 all-to-all-start.1
  41.1 3.1 dynamic-slice_reduce_fusion
  47.4 11.2 %all-gather.21.cloned.1.call-done = bf16[1024,512]{1,0:T(8,128)(2,1)} async-done(((bf16[32,512]{1,0:T(8,128)(2,1)}), bf16[1024,512]{1,0:T(8,128)(2,1)}) %all-gather.21.cloned.1.call-update) | async-done | bytes 1048592 | tf_op jit(solution)/shard_map/all_gather | solution.py:19
  58.6 2.9 gather_fusion.20
  64.4 6.3 gather_fusion.1
  70.7 4.9 add_convert_fusion.9
  81.7 41.6 %all-gather.23.cloned.1.call-done = bf16[1024,512]{1,0:T(8,128)(2,1)} async-done(((bf16[32,512]{1,0:T(8,128)(2,1)}), bf16[1024,512]{1,0:T(8,128)(2,1)}) %all-gather.23.cloned.1.call-update) | async-done | bytes 1048592 | tf_op jit(solution)/shard_map/all_gather | solution.py:19
  129.2 6.3 gather_fusion.3
  135.5 4.9 add_convert_fusion.8
  146.5 36.4 %collective-permute-done = bf16[1536,512]{1,0:T(8,128)(2,1)S(1)} collective-permute-done((bf16[1536,512]{1,0:T(8,128)(2,1)S(1)}, bf16[1536,512]{1,0:T(8,128)(2,1)S(1)}, u32[]{:S(2)}, u32[]{:S(2)}) %collective-permute-start) | collective-permute-done | bytes 1572896 | tf_op jit(solution)/shard_map/ppermute | solution.py:13
  188.0 42.1 %all-gather.25.cloned.1.call-done = bf16[1024,512]{1,0:T(8,128)(2,1)} async-done(((bf16[32,512]{1,0:T(8,128)(2,1)}), bf16[1024,512]{1,0:T(8,128)(2,1)}) %all-gather.25.cloned.1.call-update) | async-done | bytes 1048592 | tf_op jit(solution)/shard_map/all_gather | solution.py:19
  236.0 6.3 gather_fusion.5
  242.3 4.9 add_convert_fusion.7
  253.5 42.3 %all-gather.27.cloned.1.call-done = bf16[1024,512]{1,0:T(8,128)(2,1)} async-done(((bf16[32,512]{1,0:T(8,128)(2,1)}), bf16[1024,512]{1,0:T(8,128)(2,1)}) %all-gather.27.cloned.1.call-update) | async-done | bytes 1048592 | tf_op jit(solution)/shard_map/all_gather | solution.py:19
  301.6 6.3 gather_fusion.7
  307.9 4.9 add_convert_fusion.6
  314.1 3.9 fusion.52
  319.7 36.0 %collective-permute-done.1 = bf16[1536,512]{1,0:T(8,128)(2,1)S(1)} collective-permute-done((bf16[1536,512]{1,0:T(8,128)(2,1)S(1)}, bf16[1536,512]{1,0:T(8,128)(2,1)S(1)}, u32[]{:S(2)}, u32[]{:S(2)}) %collective-permute-start.1) | collective-permute-done | bytes 1572896 | tf_op jit(solution)/shard_map/ppermute | solution.py:13
  360.5 42.5 %all-gather.29.cloned.1.call-done = bf16[1024,512]{1,0:T(8,128)(2,1)} async-done(((bf16[32,512]{1,0:T(8,128)(2,1)}), bf16[1024,512]{1,0:T(8,128)(2,1)}) %all-gather.29.cloned.1.call-update) | async-done | bytes 1048592 | tf_op jit(solution)/shard_map/all_gather | solution.py:19
  408.7 6.3 gather_fusion.9
  415.1 4.9 add_convert_fusion.5
  426.3 42.3 %all-gather.31.cloned.1.call-done = bf16[1024,512]{1,0:T(8,128)(2,1)} async-done(((bf16[32,512]{1,0:T(8,128)(2,1)}), bf16[1024,512]{1,0:T(8,128)(2,1)}) %all-gather.31.cloned.1.call-update) | async-done | bytes 1048592 | tf_op jit(solution)/shard_map/all_gather | solution.py:19
  474.4 6.3 gather_fusion.11
  480.7 4.9 add_convert_fusion.4
  486.9 3.9 fusion.49
  492.3 36.2 %collective-permute-done.2 = bf16[1536,512]{1,0:T(8,128)(2,1)S(1)} collective-permute-done((bf16[1536,512]{1,0:T(8,128)(2,1)S(1)}, bf16[1536,512]{1,0:T(8,128)(2,1)S(1)}, u32[]{:S(2)}, u32[]{:S(2)}) %collective-permute-start.2) | collective-permute-done | bytes 1572896 | tf_op jit(solution)/shard_map/ppermute | solution.py:13
  533.4 42.3 %all-gather.33.cloned.1.call-done = bf16[1024,512]{1,0:T(8,128)(2,1)} async-done(((bf16[32,512]{1,0:T(8,128)(2,1)}), bf16[1024,512]{1,0:T(8,128)(2,1)}) %all-gather.33.cloned.1.call-update) | async-done | bytes 1048592 | tf_op jit(solution)/shard_map/all_gather | solution.py:19
  575.7 2.9 gather_fusion.26
  581.5 6.3 gather_fusion.13
  587.8 4.9 add_convert_fusion.3
  599.1 42.2 %all-gather.35.cloned.1.call-done = bf16[1024,512]{1,0:T(8,128)(2,1)} async-done(((bf16[32,512]{1,0:T(8,128)(2,1)}), bf16[1024,512]{1,0:T(8,128)(2,1)}) %all-gather.35.cloned.1.call-update) | async-done | bytes 1048592 | tf_op jit(solution)/shard_map/all_gather | solution.py:19
  641.4 2.9 gather_fusion.27
  647.2 6.3 gather_fusion.15
  653.5 4.9 add_convert_fusion.2
  659.6 3.9 fusion.46
  664.9 36.3 %collective-permute-done.3 = bf16[1536,512]{1,0:T(8,128)(2,1)S(1)} collective-permute-done((bf16[1536,512]{1,0:T(8,128)(2,1)S(1)}, bf16[1536,512]{1,0:T(8,128)(2,1)S(1)}, u32[]{:S(2)}, u32[]{:S(2)}) %collective-permute-start.3) | collective-permute-done | bytes 1572896 | tf_op jit(solution)/shard_map/ppermute | solution.py:13
  706.2 42.3 %all-gather.37.cloned.1.call-done = bf16[1024,512]{1,0:T(8,128)(2,1)} async-done(((bf16[32,512]{1,0:T(8,128)(2,1)}), bf16[1024,512]{1,0:T(8,128)(2,1)}) %all-gather.37.cloned.1.call-update) | async-done | bytes 1048592 | tf_op jit(solution)/shard_map/all_gather | solution.py:19
  748.5 2.9 gather_fusion.28
  754.3 6.3 gather_fusion.17
  760.6 4.9 add_convert_fusion.1
  771.9 3.8 copy.136
  775.7 38.5 %all-gather.39.cloned.1.call-done = bf16[1024,512]{1,0:T(8,128)(2,1)} async-done(((bf16[32,512]{1,0:T(8,128)(2,1)}), bf16[1024,512]{1,0:T(8,128)(2,1)}) %all-gather.39.cloned.1.call-update) | async-done | bytes 1048592 | tf_op jit(solution)/shard_map/all_gather | solution.py:19
  814.2 3.0 gather_fusion.29
  820.1 6.3 gather_fusion.19
  826.4 4.9 add_convert_fusion
  832.5 3.8 fusion.43
  (188 shorter events, 121.4 us)
Async XLA Ops:
  6.5 64.2 %copy-start = (bf16[2,12,4,128,128]{4,3,2,1,0:T(8,128)(2,1)S(1)}, bf16[2,12,4,128,128]{4,3,2,1,0:T(8,128)(2,1)}, u32[]{:S(2)}) copy-start(bf16[2,12,4,128,128]{4,3,2,1,0:T(8,128)(2,1)} %param.11) | copy-start | bytes 9437188
  6.5 6.6 copy-start.23
  6.5 16.2 %copy-start.22 = (s32[2,32,8]{1,2,0:T(8,128)S(1)}, s32[2,32,8]{1,2,0:T(8,128)}, u32[]{:S(2)}) copy-start(s32[2,32,8]{1,2,0:T(8,128)} %param.14) | copy-start | bytes 6148
  6.5 16.9 %copy-start.21 = (s32[2,12,4]{1,2,0:T(4,128)S(1)}, s32[2,12,4]{1,2,0:T(4,128)}, u32[]{:S(2)}) copy-start(s32[2,12,4]{1,2,0:T(4,128)} %param.12) | copy-start | bytes 1156
  6.5 52.0 %all-gather.21.cloned.1.call-start = ((), (), s32[]{:S(2)}) async-start(), calls=%async_computation.2 | async-start | bytes 1081344 | tf_op jit(solution)/shard_map/all_gather | solution.py:19
  13.8 19.5 %all-to-all-start = ((s32[2,32,1]{0,2,1:T(1,128)}), s32[2,32,1]{0,2,1:T(1,128)S(1)}, u32[]{:S(2)}, u32[]{:S(2)}) async-start(s32[2,32,1]{0,2,1:T(1,128)} %copy.85), calls=%async_computation | async-start | bytes 32768 | tf_op jit(solution)/shard_map/all_to_all | solution.py:48
  33.4 13.6 %all-to-all-start.1 = ((s32[2,32,8]{2,0,1:T(2,128)}), s32[2,32,8]{2,0,1:T(2,128)S(1)}, u32[]{:S(2)}, u32[]{:S(2)}) async-start(s32[2,32,8]{2,0,1:T(2,128)} %copy.86), calls=%async_computation.1 | async-start | bytes 65536 | tf_op jit(solution)/shard_map/all_to_all | solution.py:47
  40.8 82.6 %all-gather.23.cloned.1.call-start = ((), (), s32[]{:S(2)}) async-start(), calls=%async_computation.3 | async-start | bytes 1081344 | tf_op jit(solution)/shard_map/all_gather | solution.py:19
  70.7 4.9 copy-start.1
  70.7 4.9 copy-start.11
  81.1 149.1 %all-gather.25.cloned.1.call-start = ((), (), s32[]{:S(2)}) async-start(), calls=%async_computation.4 | async-start | bytes 1081344 | tf_op jit(solution)/shard_map/all_gather | solution.py:19
  135.5 4.9 copy-start.2
  141.0 1.9 copy-start.12
  145.2 37.7 %collective-permute-start = (bf16[1536,512]{1,0:T(8,128)(2,1)S(1)}, bf16[1536,512]{1,0:T(8,128)(2,1)S(1)}, u32[]{:S(2)}, u32[]{:S(2)}) collective-permute-start(bf16[1536,512]{1,0:T(8,128)(2,1)S(1)} %get-tuple-element.36), channel_id=1, source_target_pairs={{0,32},{32,64},{64,96},{1,33},{33,65},{65,97},{2,34},{34,66},{66,9... | collective-permute-start | bytes 4718600 | tf_op jit(solution)/shard_map/ppermute | solution.py:13
  187.1 108.7 %all-gather.27.cloned.1.call-start = ((), (), s32[]{:S(2)}) async-start(), calls=%async_computation.5 | async-start | bytes 1081344 | tf_op jit(solution)/shard_map/all_gather | solution.py:19
  242.3 4.9 copy-start.3
  247.2 1.2 copy-start.13
  253.5 149.4 %all-gather.29.cloned.1.call-start = ((), (), s32[]{:S(2)}) async-start(), calls=%async_computation.6 | async-start | bytes 1081344 | tf_op jit(solution)/shard_map/all_gather | solution.py:19
  307.9 4.9 copy-start.4
  312.9 1.2 copy-start.14
  318.0 37.7 %collective-permute-start.1 = (bf16[1536,512]{1,0:T(8,128)(2,1)S(1)}, bf16[1536,512]{1,0:T(8,128)(2,1)S(1)}, u32[]{:S(2)}, u32[]{:S(2)}) collective-permute-start(bf16[1536,512]{1,0:T(8,128)(2,1)S(1)} %get-tuple-element.42), channel_id=1, source_target_pairs={{0,32},{32,64},{64,96},{1,33},{33,65},{65,97},{2,34},{34,66},{66,9... | collective-permute-start | bytes 4718600 | tf_op jit(solution)/shard_map/ppermute | solution.py:13
  359.9 108.7 %all-gather.31.cloned.1.call-start = ((), (), s32[]{:S(2)}) async-start(), calls=%async_computation.7 | async-start | bytes 1081344 | tf_op jit(solution)/shard_map/all_gather | solution.py:19
  415.1 4.9 copy-start.5
  420.0 1.2 copy-start.15
  426.3 149.4 %all-gather.33.cloned.1.call-start = ((), (), s32[]{:S(2)}) async-start(), calls=%async_computation.8 | async-start | bytes 1081344 | tf_op jit(solution)/shard_map/all_gather | solution.py:19
  480.7 4.9 copy-start.6
  485.6 1.2 copy-start.16
  490.8 37.7 %collective-permute-start.2 = (bf16[1536,512]{1,0:T(8,128)(2,1)S(1)}, bf16[1536,512]{1,0:T(8,128)(2,1)S(1)}, u32[]{:S(2)}, u32[]{:S(2)}) collective-permute-start(bf16[1536,512]{1,0:T(8,128)(2,1)S(1)} %get-tuple-element.48), channel_id=1, source_target_pairs={{0,32},{32,64},{64,96},{1,33},{33,65},{65,97},{2,34},{34,66},{66,9... | collective-permute-start | bytes 4718600 | tf_op jit(solution)/shard_map/ppermute | solution.py:13
  532.6 108.7 %all-gather.35.cloned.1.call-start = ((), (), s32[]{:S(2)}) async-start(), calls=%async_computation.9 | async-start | bytes 1081344 | tf_op jit(solution)/shard_map/all_gather | solution.py:19
  587.8 4.9 copy-start.7
  592.8 1.2 copy-start.17
  599.1 149.5 %all-gather.37.cloned.1.call-start = ((), (), s32[]{:S(2)}) async-start(), calls=%async_computation.10 | async-start | bytes 1081344 | tf_op jit(solution)/shard_map/all_gather | solution.py:19
  653.5 4.9 copy-start.8
  658.4 1.2 copy-start.18
  663.5 37.6 %collective-permute-start.3 = (bf16[1536,512]{1,0:T(8,128)(2,1)S(1)}, bf16[1536,512]{1,0:T(8,128)(2,1)S(1)}, u32[]{:S(2)}, u32[]{:S(2)}) collective-permute-start(bf16[1536,512]{1,0:T(8,128)(2,1)S(1)} %get-tuple-element.54), channel_id=1, source_target_pairs={{0,32},{32,64},{64,96},{1,33},{33,65},{65,97},{2,34},{34,66},{66,9... | collective-permute-start | bytes 4718600 | tf_op jit(solution)/shard_map/ppermute | solution.py:13
  705.4 108.8 %all-gather.39.cloned.1.call-start = ((), (), s32[]{:S(2)}) async-start(), calls=%async_computation.11 | async-start | bytes 1081344 | tf_op jit(solution)/shard_map/all_gather | solution.py:19
  760.6 4.9 copy-start.9
  765.6 1.2 copy-start.19
  826.4 4.9 copy-start.10
  831.3 1.2 copy-start.20
Sparse Core Ops, SparseCore 0:
  13.3 45.2 all-gather.20
  81.2 42.1 all-gather.22
  187.2 42.8 all-gather.24
  253.6 42.1 all-gather.26
  360.0 42.8 all-gather.28
  426.4 42.1 all-gather.30
  532.8 42.8 all-gather.32
  599.2 42.1 all-gather.34
  705.5 42.9 all-gather.36
  772.0 42.1 all-gather.38
where the time goes:
time: 850 us; the launch traced here: 843 us
  waiting for transfers between devices  535 us (63%)
  local copies, waits for them, and re-layouts  139 us (16%)
  matrix products  78.2 us (9%)
  other arithmetic  53 us (6%)
  starting transfers between devices  23.6 us (3%)
  between operations  14.7 us (2%)
    all_gather x10, waiting for transfers between devices, halo_rows(): everyone = lax.all_gather(picked, 'dom', axis=0, tiled=True)  387 us
    ppermute x4, waiting for transfers between devices, passed_along(): return lax.ppermute(x, axis, pairs)  145 us
    gather x10, local copies, waits for them, and re-layouts, mix_layer(): blocks = table[column_ids]  63.2 us
    dot_general x10, matrix products, mix_layer(): jnp.einsum('rkij,rkjd->rid', tile_block, blocks, preferred_element_type=j...  49 us
    gather x20, local copies, waits for them, and re-layouts, halo_rows(): chosen = jnp.take_along_axis(everyone, positions[:, :, None], axis=1)  30 us
    dot_general x10, matrix products, mix_layer(): product = jnp.dot(zround, weight, preferred_element_type=jnp.float32)  29.2 us
    gather x10, local copies, waits for them, and re-layouts, halo_rows(): picked = features[bound_idx]  28.5 us
    concatenate x10, other arithmetic, mix_layer(): jnp.concatenate([features, extra, jnp.zeros((spare, width), features.dtyp...  27.6 us
  transfers between devices with their start and end apart: 16, of which 15 were waited for; matrix products, arithmetic and copies ran while one was open for 2% of the time, Pallas kernels for 0%

commit v1 on v0

v1 whole, which is shorter than its diff:
```python
import math
import jax
import jax.numpy as jnp
from jax import lax
from jax.experimental import pallas as pl
from jax.experimental.pallas import tpu as pltpu
from jax.sharding import PartitionSpec as P

restart_share = 0.1
decay_scale = 1.0
f32 = jnp.float32
bf16 = jnp.bfloat16


def dot(a, b):
    return jnp.dot(a, b, preferred_element_type=f32)


def whole(*shape):
    return pl.BlockSpec(shape, lambda: (0,) * len(shape))


def pick_kernel(h0_ref, rows_ref, slots_ref, send_ref, picked_ref):
    batches, bound, _ = rows_ref.shape
    picked = []
    for b in range(batches):
        picked.append(dot(rows_ref[b], h0_ref[b]))
    picked = jnp.concatenate(picked, 0)
    picked_ref[...] = restart_share * picked
    send_ref[...] = dot(slots_ref[...], picked.astype(bf16)).astype(bf16)


def spread_of(b, batches, rows, cap):
    row = lax.broadcasted_iota(jnp.int32, (rows, rows * batches), 0)
    col = lax.broadcasted_iota(jnp.int32, (rows, rows * batches), 1)
    hit = col == (row // cap) * (cap * batches) + b * cap + row % cap
    return jnp.where(hit, 1.0, 0.0).astype(bf16)


def bound_kernel(cap, cols_ref, h0_ref, rows_ref, vals_ref, picked_ref, local_ref, halo_ref, part_ref, acc_ref):
    batches, bound, nodes = rows_ref.shape
    _, row_tiles, kt, tile, _ = vals_ref.shape
    halo = halo_ref.shape[1] // batches
    for b in range(batches):
        acc_ref[...] = jnp.zeros_like(acc_ref)
        for r in range(row_tiles):
            sel = rows_ref[b, :, r * tile:(r + 1) * tile]
            for k in range(kt):
                c = cols_ref[(b * row_tiles + r) * kt + k]
                acc_ref[c] += dot(sel, vals_ref[b, r, k])
        local = jnp.concatenate([acc_ref[t] for t in range(row_tiles)], 1).astype(bf16)
        rest = jnp.concatenate([acc_ref[t] for t in range(row_tiles, acc_ref.shape[0])], 1).astype(bf16)
        local_ref[b] = local
        halo_ref[b * bound:(b + 1) * bound, :] = dot(rest, spread_of(b, batches, halo, cap)).astype(bf16)
        part_ref[b * bound:(b + 1) * bound, :] = (
            (1.0 - restart_share) * dot(local, h0_ref[b]) + picked_ref[b * bound:(b + 1) * bound, :])


def edge_kernel(beta, part_ref, halo_ref, recv_ref, w_ref, slots_ref, send_ref):
    z = part_ref[...] + (1.0 - restart_share) * dot(halo_ref[...], recv_ref[...])
    prod = dot(z.astype(bf16), w_ref[...])
    h = jnp.maximum((1.0 - beta) * z + beta * prod, 0.0).astype(bf16)
    send_ref[...] = dot(slots_ref[...], h).astype(bf16)


def bulk_kernel(beta, first_live, cap, meta_ref, x_ref, recv_ref, vals_ref, h0_ref, w_ref, local_ref, picked_ref,
                h_ref, part_ref, table_ref):
    b, g = pl.program_id(0), pl.program_id(1)
    batches = pl.num_programs(0)
    _, tiles, kt, tile, _ = vals_ref.shape
    row_tiles = tiles * pl.num_programs(1)
    nodes = x_ref.shape[1]
    rows = tiles * tile
    live = meta_ref[0] >= first_live

    @pl.when(jnp.logical_not(live))
    def _():
        h_ref[0] = x_ref[0, pl.ds(pl.multiple_of(g * rows, rows), rows), :]
        part_ref[...] = jnp.zeros_like(part_ref)

    @pl.when(live & (g == 0))
    def _():
        for t in range(nodes // tile):
            table_ref[t] = x_ref[0, t * tile:(t + 1) * tile, :]
        halo = table_ref.shape[0] * tile - nodes
        spread = spread_of(b, recv_ref.shape[0] // halo, halo, cap)
        got = dot(spread, recv_ref[...]).astype(bf16)
        for t in range(halo // tile):
            table_ref[nodes // tile + t] = got[t * tile:(t + 1) * tile]
        part_ref[0] = picked_ref[0]

    @pl.when(live)
    def _():
        zs = []
        for r in range(tiles):
            base = 1 + (b * row_tiles + g * tiles + r) * kt
            lhs = jnp.concatenate([vals_ref[0, r, k] for k in range(kt)], 1)
            rhs = jnp.concatenate([table_ref[meta_ref[base + k]] for k in range(kt)], 0)
            zs.append(dot(lhs, rhs))
        z = (1.0 - restart_share) * jnp.concatenate(zs, 0) + restart_share * h0_ref[0].astype(f32)
        prod = dot(z.astype(bf16), w_ref[...])
        h = jnp.maximum((1.0 - beta) * z + beta * prod, 0.0).astype(bf16)
        h_ref[0] = h
        part_ref[0] += (1.0 - restart_share) * dot(local_ref[0], h)


def params(**kw):
    return pltpu.CompilerParams(vmem_limit_bytes=28 * 1024 * 1024, **kw)


def cost(flops, nbytes):
    return pl.CostEstimate(flops=int(flops), bytes_accessed=int(nbytes), transcendentals=0)


def body(h0, layer_weight, tile_vals, tile_cols, boundary, send_pos, send_count):
    sections = lax.axis_size("section")
    place = lax.axis_index("section").astype(jnp.int32)
    batches, nodes, width = h0.shape
    depth = layer_weight.shape[0]
    layers = depth * sections
    _, row_tiles, kt, tile, _ = tile_vals.shape
    bound = boundary.shape[1]
    doms, cap = send_pos.shape[1], send_pos.shape[2]
    halo = doms * cap
    all_tiles = (nodes + halo + tile - 1) // tile
    groups = 3
    rows = nodes // groups

    turned = [[layer_weight[i] for i in range(depth)]]
    for i in range(depth):
        for k in range(1, sections):
            if i == 0:
                turned.append([None] * depth)
            turned[k][i] = lax.ppermute(layer_weight[i], "section", [(s, (s + k) % sections) for s in range(sections)])

    def weight_of(layer):
        s, i = layer // depth, layer % depth
        turn = (place - s) % sections
        w = turned[0][i]
        for k in range(1, sections):
            w = jnp.where(turn == k, turned[k][i], w)
        return w

    node_id = jnp.arange(nodes, dtype=jnp.int32)
    rows_sel = (boundary[:, :, None] == node_id[None, None, :]).astype(bf16)
    live = jnp.arange(cap, dtype=jnp.int32)[None, None, :] < send_count[:, :, None]
    slot = jnp.where(live, send_pos + bound * jnp.arange(batches, dtype=jnp.int32)[:, None, None], -1)
    slot = jnp.transpose(slot, (1, 0, 2)).reshape(doms * batches * cap)
    slots_sel = (slot[:, None] == jnp.arange(batches * bound, dtype=jnp.int32)[None, :]).astype(bf16)
    cols = tile_cols.reshape(-1).astype(jnp.int32)
    meta = jnp.concatenate([place[None], cols])

    lines = doms * batches * cap

    def exchanged(x):
        return lax.all_to_all(x, "dom", split_axis=0, concat_axis=0, tiled=True)

    send, picked = pl.pallas_call(
        pick_kernel,
        out_shape=(jax.ShapeDtypeStruct((lines, width), bf16), jax.ShapeDtypeStruct((batches * bound, width), f32)),
        compiler_params=params(),
        name="pick",
    )(h0, rows_sel, slots_sel)
    recv = exchanged(send)

    local, halo_sel, part = pl.pallas_call(
        lambda *refs: bound_kernel(cap, *refs),
        in_specs=[pl.BlockSpec(memory_space=pltpu.SMEM)] + [pl.BlockSpec(memory_space=pltpu.VMEM)] * 4,
        out_shape=(
            jax.ShapeDtypeStruct((batches, bound, nodes), bf16),
            jax.ShapeDtypeStruct((batches * bound, lines), bf16),
            jax.ShapeDtypeStruct((batches * bound, width), f32),
        ),
        scratch_shapes=[pltpu.VMEM((all_tiles, bound, tile), f32)],
        compiler_params=params(),
        cost_estimate=cost(4e9, 8e6),
        name="bound",
    )(cols, h0, rows_sel, tile_vals, picked)
    picked3 = picked.reshape(batches, bound, width)

    def edge(part, recv, w, beta):
        return pl.pallas_call(
            lambda *refs: edge_kernel(beta, *refs),
            out_shape=jax.ShapeDtypeStruct((lines, width), bf16),
            compiler_params=params(),
            cost_estimate=cost(1e8, 2e6),
            name="edge",
        )(part, halo_sel, recv, w, slots_sel)

    def bulk(x, recv, w, beta, first_live):
        h, part = pl.pallas_call(
            lambda *refs: bulk_kernel(beta, first_live, cap, *refs),
            grid_spec=pltpu.PrefetchScalarGridSpec(
                num_scalar_prefetch=1,
                grid=(batches, groups),
                in_specs=[
                    pl.BlockSpec((1, nodes, width), lambda b, g, m: (b, 0, 0)),
                    pl.BlockSpec((lines, width), lambda b, g, m: (0, 0)),
                    pl.BlockSpec((1, row_tiles // groups, kt, tile, tile), lambda b, g, m: (b, g, 0, 0, 0)),
                    pl.BlockSpec((1, rows, width), lambda b, g, m: (b, g, 0)),
                    pl.BlockSpec((width, width), lambda b, g, m: (0, 0)),
                    pl.BlockSpec((1, bound, rows), lambda b, g, m: (b, 0, g)),
                    pl.BlockSpec((1, bound, width), lambda b, g, m: (b, 0, 0)),
                ],
                out_specs=[
                    pl.BlockSpec((1, rows, width), lambda b, g, m: (b, g, 0)),
                    pl.BlockSpec((1, bound, width), lambda b, g, m: (b, 0, 0)),
                ],
                scratch_shapes=[pltpu.VMEM((all_tiles, tile, width), bf16)],
            ),
            out_shape=(
                jax.ShapeDtypeStruct((batches, nodes, width), bf16),
                jax.ShapeDtypeStruct((batches, bound, width), f32),
            ),
            compiler_params=params(dimension_semantics=("arbitrary", "arbitrary")),
            cost_estimate=cost(7e9, 16e6),
            name="bulk",
        )(meta, x, recv, tile_vals, h0, w, local, picked3)
        return h, part.reshape(batches * bound, width)

    x = h0
    for layer in range(layers):
        beta = math.log(decay_scale / (layer + 1) + 1.0)
        w = weight_of(layer)
        ahead = None
        if layer + 1 < layers:
            ahead = exchanged(edge(part, recv, w, beta))
        x, part = bulk(x, recv, w, beta, layer // depth)
        recv = ahead
    return x[None]


def solution(mesh):
    placed = (
        P(None, "dom", None),
        P("section", None, None),
        P(None, "dom", None, None, None),
        P(None, "dom", None),
        P(None, "dom"),
        P(None, "dom", None),
        P(None, "dom"),
    )
    return jax.shard_map(
        body, mesh=mesh, in_specs=placed, out_specs=P("section", None, "dom", None), check_vma=False
    )
```

time: 850 us -> 256 us (0.30)
  waiting for transfers between devices: 535 us -> 10.5 us
  Pallas kernels: 0 us -> 81.5 us
  matrix products: 78.2 us -> 0 us
  local copies, waits for them, and re-layouts: 139 us -> 84 us
  other arithmetic: 53 us -> 7.59 us
  starting transfers between devices: 23.6 us -> 68.7 us
  between operations: 14.7 us -> 0.5 us
    all_gather x10 -> x0, waiting for transfers between devices: 387 us -> none  [halo_rows(): everyone = lax.all_gather(picked, 'dom', axis=0, tiled=True)]
    ppermute x4 -> x6, waiting for transfers between devices: 145 us -> 10.4 us  [body(): lax.ppermute(layer_weight[i], 'section', [(s, (s + k) % sections) for s i...]
    gather x40 -> x0, local copies, waits for them, and re-layouts: 122 us -> none  [the longest x10 63.2 us: mix_layer(): blocks = table[column_ids]]
    pallas_call x0 -> x17, Pallas kernels: none -> 81.5 us  [the longest x8 66.6 us: bulk(): pl.pallas_call(lambda *refs: bulk_kernel(beta, first_live, cap, *refs), g...]
    dot_general x20 -> x0, matrix products: 78.2 us -> none  [the longest x10 49 us: mix_layer(): jnp.einsum('rkij,rkjd->rid', tile_block, blocks, preferred_element_type=j...]
    unnamed x55 -> x141, local copies, waits for them, and re-layouts: 10.1 us -> 81.4 us
    all_to_all x2 -> x8, starting transfers between devices: 16.3 us -> 63.7 us  [exchanged(): return lax.all_to_all(x, 'dom', split_axis=0, concat_axis=0, tiled=True)]
    concatenate x10 -> x1, other arithmetic: 27.6 us -> 0.07 us  [body(): meta = jnp.concatenate([place[None], cols])]
  transfers between devices with their start and end apart: 16 -> 14, of which waited for: 15 -> 2; matrix products, arithmetic and copies ran while one was open for 2% -> 3% of each run, Pallas kernels for 0% -> 25%
where the time goes in v1:
time: 256 us; the launch traced here: 253 us
  local copies, waits for them, and re-layouts  84 us (33%)
  Pallas kernels  81.5 us (32%)
  starting transfers between devices  68.7 us (27%)
  waiting for transfers between devices  10.5 us (4%)
  other arithmetic  7.59 us (3%)
    unnamed x141, local copies, waits for them, and re-layouts  81.4 us
    pallas_call x8, Pallas kernels, bulk(): pl.pallas_call(lambda *refs: bulk_kernel(beta, first_live, cap, *refs), g...  66.6 us
    all_to_all x8, starting transfers between devices, exchanged(): return lax.all_to_all(x, 'dom', split_axis=0, concat_axis=0, tiled=True)  63.7 us
    pallas_call x7, Pallas kernels, edge(): pl.pallas_call(lambda *refs: edge_kernel(beta, *refs), out_shape=jax.Shap...  11.7 us
    ppermute x6, waiting for transfers between devices, body(): lax.ppermute(layer_weight[i], 'section', [(s, (s + k) % sections) for s i...  10.4 us
    select_n x2, other arithmetic, weight_of(): w = jnp.where(turn == k, turned[k][i], w)  5.83 us
  transfers between devices with their start and end apart: 14, of which 2 were waited for; matrix products, arithmetic and copies ran while one was open for 3% of the time, Pallas kernels for 25%

profile of v1, /device:TPU:15, one launch (start us, length us, event | category | flops | bytes accessed | tf_op | source)
XLA Modules:
  0.0 252.7 jit_solution(11512988758122353521)
XLA Ops:
  0.0 2.2 slice_bitcast_fusion
  2.5 2.1 collective-permute-start.4
  8.6 1.9 copy-done
  12.9 10.0 %all-to-all-start = ((bf16[32,16,512]{2,1,0:T(8,128)(2,1)}), bf16[32,16,512]{2,1,0:T(8,128)(2,1)}, u32[]{:S(2)}, u32[]{:S(2)}) async-start(bf16[32,16,512]{2,1,0:T(8,128)(2,1)} %bitcast.54), calls=%async_computation | async-start | bytes 1048576 | tf_op jit(solution)/shard_map/all_to_all | solution.py:156
  23.2 1.9 copy-done.27
  25.9 2.3 bound.1
  29.7 8.2 %collective-permute-done.2 = bf16[512,512]{1,0:T(8,128)(2,1)} collective-permute-done((bf16[512,512]{1,0:T(8,128)(2,1)}, bf16[512,512]{1,0:T(8,128)(2,1)}, u32[]{:S(2)}, u32[]{:S(2)}) %collective-permute-start.2) | collective-permute-done | bytes 524320 | tf_op jit(solution)/shard_map/ppermute | solution.py:134
  38.4 2.2 collective-permute-done
  40.6 3.0 %select_select_fusion.1 = (bf16[512,512]{1,0:T(8,128)(2,1)}, bf16[512,512]{1,0:T(8,128)(2,1)}, bf16[512,512]{1,0:T(8,128)(2,1)}, bf16[512,512]{1,0:T(8,128)(2,1)}) fusion(bf16[512,512]{1,0:T(8,128)(2,1)} %collective-permute-done, bf16[512,512]{1,0:T(8,128)(2,1)} %collective-permute-done.1, bf16[512,512]{1,0:T(8,128)(2,1)} %collective-permute-done.2, ...), kind=kLoop, calls=%fused_computation.1 | loop fusion | flops 3145728 | bytes 4194316 | tf_op jit(solution)/shard_map/jit(_where)/select_n | solution.py:141
  44.6 1.7 edge.7
  47.1 9.0 %all-to-all-start.1 = ((bf16[32,16,512]{2,1,0:T(8,128)(2,1)}), bf16[32,16,512]{2,1,0:T(8,128)(2,1)}, u32[]{:S(2)}, u32[]{:S(2)}) async-start(bf16[32,16,512]{2,1,0:T(8,128)(2,1)} %bitcast.47), calls=%async_computation.1 | async-start | bytes 1048576 | tf_op jit(solution)/shard_map/all_to_all | solution.py:156
  57.2 1.9 copy-done.28
  60.9 8.1 %bulk.8 = (bf16[2,1536,512]{2,1,0:T(8,128)(2,1)S(1)}, f32[2,32,512]{2,1,0:T(8,128)S(1)}) custom-call(s32[97]{0:T(128)S(1)} %pad_add_fusion.refs_0_, bf16[2,1536,512]{2,1,0:T(8,128)(2,1)S(1)} %copy-done.1, bf16[512,512]{1,0:T(8,128)(2,1)} %bitcast.3.refs_2_, bf16[2,12,4,128,128]{4,3,2,1,0:T(8,128)(2,1)S(1)} %copy-done.28, ...), custom_call_target="tpu_custom_call" | custom-call | flops 7000000000 | bytes 16000000 | tf_op jit(solution)/shard_map/bulk/pallas_call | solution.py:191
  70.7 2.8 %select_select_fusion = (bf16[512,512]{1,0:T(8,128)(2,1)}, bf16[512,512]{1,0:T(8,128)(2,1)}, bf16[512,512]{1,0:T(8,128)(2,1)}, bf16[512,512]{1,0:T(8,128)(2,1)}) fusion(bf16[512,512]{1,0:T(8,128)(2,1)} %collective-permute-done.3, bf16[512,512]{1,0:T(8,128)(2,1)} %collective-permute-done.4, bf16[512,512]{1,0:T(8,128)(2,1)} %collective-permute-done.5, ...), kind=kLoop, calls=%fused_computation | loop fusion | flops 3145728 | bytes 4194316 | tf_op jit(solution)/shard_map/jit(_where)/select_n | solution.py:141
  74.6 1.7 edge.8
  77.1 7.5 %all-to-all-start.2 = ((bf16[32,16,512]{2,1,0:T(8,128)(2,1)}), bf16[32,16,512]{2,1,0:T(8,128)(2,1)}, u32[]{:S(2)}, u32[]{:S(2)}) async-start(bf16[32,16,512]{2,1,0:T(8,128)(2,1)} %bitcast.49), calls=%async_computation.2 | async-start | bytes 1048576 | tf_op jit(solution)/shard_map/all_to_all | solution.py:156
  85.6 1.9 copy-done.29
  88.4 1.9 copy-done.47
  91.2 8.1 %bulk.9 = (bf16[2,1536,512]{2,1,0:T(8,128)(2,1)S(1)}, f32[2,32,512]{2,1,0:T(8,128)S(1)}) custom-call(s32[97]{0:T(128)S(1)} %pad_add_fusion.refs_0_, bf16[2,1536,512]{2,1,0:T(8,128)(2,1)S(1)} %copy-done.47, bf16[512,512]{1,0:T(8,128)(2,1)} %bitcast.7.refs_2_, bf16[2,12,4,128,128]{4,3,2,1,0:T(8,128)(2,1)S(1)} %copy-done.29, ...), custom_call_target="tpu_custom_call" | custom-call | flops 7000000000 | bytes 16000000 | tf_op jit(solution)/shard_map/bulk/pallas_call | solution.py:191
  102.0 1.7 edge.9
  104.5 7.4 %all-to-all-start.3 = ((bf16[32,16,512]{2,1,0:T(8,128)(2,1)}), bf16[32,16,512]{2,1,0:T(8,128)(2,1)}, u32[]{:S(2)}, u32[]{:S(2)}) async-start(bf16[32,16,512]{2,1,0:T(8,128)(2,1)} %bitcast.50), calls=%async_computation.3 | async-start | bytes 1048576 | tf_op jit(solution)/shard_map/all_to_all | solution.py:156
  113.0 1.9 copy-done.30
  115.8 1.9 copy-done.51
  118.6 8.1 %bulk.10 = (bf16[2,1536,512]{2,1,0:T(8,128)(2,1)S(1)}, f32[2,32,512]{2,1,0:T(8,128)S(1)}) custom-call(s32[97]{0:T(128)S(1)} %pad_add_fusion.refs_0_, bf16[2,1536,512]{2,1,0:T(8,128)(2,1)S(1)} %copy-done.51, bf16[512,512]{1,0:T(8,128)(2,1)} %bitcast.11.refs_2_, bf16[2,12,4,128,128]{4,3,2,1,0:T(8,128)(2,1)S(1)} %copy-done.30, ...), custom_call_target="tpu_custom_call" | custom-call | flops 7000000000 | bytes 16000000 | tf_op jit(solution)/shard_map/bulk/pallas_call | solution.py:191
  129.4 1.7 edge.10
  131.9 7.5 %all-to-all-start.4 = ((bf16[32,16,512]{2,1,0:T(8,128)(2,1)}), bf16[32,16,512]{2,1,0:T(8,128)(2,1)}, u32[]{:S(2)}, u32[]{:S(2)}) async-start(bf16[32,16,512]{2,1,0:T(8,128)(2,1)} %bitcast.51), calls=%async_computation.4 | async-start | bytes 1048576 | tf_op jit(solution)/shard_map/all_to_all | solution.py:156
  140.4 1.9 copy-done.31
  143.2 1.9 copy-done.53
  146.0 8.1 %bulk.11 = (bf16[2,1536,512]{2,1,0:T(8,128)(2,1)S(1)}, f32[2,32,512]{2,1,0:T(8,128)S(1)}) custom-call(s32[97]{0:T(128)S(1)} %pad_add_fusion.refs_0_, bf16[2,1536,512]{2,1,0:T(8,128)(2,1)S(1)} %copy-done.53, bf16[512,512]{1,0:T(8,128)(2,1)} %bitcast.14.refs_2_, bf16[2,12,4,128,128]{4,3,2,1,0:T(8,128)(2,1)S(1)} %copy-done.31, ...), custom_call_target="tpu_custom_call" | custom-call | flops 7000000000 | bytes 16000000 | tf_op jit(solution)/shard_map/bulk/pallas_call | solution.py:191
  156.8 1.7 edge.11
  159.3 7.4 %all-to-all-start.5 = ((bf16[32,16,512]{2,1,0:T(8,128)(2,1)}), bf16[32,16,512]{2,1,0:T(8,128)(2,1)}, u32[]{:S(2)}, u32[]{:S(2)}) async-start(bf16[32,16,512]{2,1,0:T(8,128)(2,1)} %bitcast.52), calls=%async_computation.5 | async-start | bytes 1048576 | tf_op jit(solution)/shard_map/all_to_all | solution.py:156
  167.8 1.9 copy-done.32
  170.6 1.9 copy-done.55
  173.4 8.1 %bulk.12 = (bf16[2,1536,512]{2,1,0:T(8,128)(2,1)S(1)}, f32[2,32,512]{2,1,0:T(8,128)S(1)}) custom-call(s32[97]{0:T(128)S(1)} %pad_add_fusion.refs_0_, bf16[2,1536,512]{2,1,0:T(8,128)(2,1)S(1)} %copy-done.55, bf16[512,512]{1,0:T(8,128)(2,1)} %bitcast.17.refs_2_, bf16[2,12,4,128,128]{4,3,2,1,0:T(8,128)(2,1)S(1)} %copy-done.32, ...), custom_call_target="tpu_custom_call" | custom-call | flops 7000000000 | bytes 16000000 | tf_op jit(solution)/shard_map/bulk/pallas_call | solution.py:191
  184.2 1.7 edge.12
  186.7 7.5 %all-to-all-start.6 = ((bf16[32,16,512]{2,1,0:T(8,128)(2,1)}), bf16[32,16,512]{2,1,0:T(8,128)(2,1)}, u32[]{:S(2)}, u32[]{:S(2)}) async-start(bf16[32,16,512]{2,1,0:T(8,128)(2,1)} %bitcast.53), calls=%async_computation.6 | async-start | bytes 1048576 | tf_op jit(solution)/shard_map/all_to_all | solution.py:156
  195.2 1.9 copy-done.33
  198.0 1.9 copy-done.57
  200.8 8.1 %bulk.13 = (bf16[2,1536,512]{2,1,0:T(8,128)(2,1)S(1)}, f32[2,32,512]{2,1,0:T(8,128)S(1)}) custom-call(s32[97]{0:T(128)S(1)} %pad_add_fusion.refs_0_, bf16[2,1536,512]{2,1,0:T(8,128)(2,1)S(1)} %copy-done.57, bf16[512,512]{1,0:T(8,128)(2,1)} %bitcast.20.refs_2_, bf16[2,12,4,128,128]{4,3,2,1,0:T(8,128)(2,1)S(1)} %copy-done.33, ...), custom_call_target="tpu_custom_call" | custom-call | flops 7000000000 | bytes 16000000 | tf_op jit(solution)/shard_map/bulk/pallas_call | solution.py:191
  211.7 1.7 edge.13
  214.1 7.4 %all-to-all-start.7 = ((bf16[32,16,512]{2,1,0:T(8,128)(2,1)}), bf16[32,16,512]{2,1,0:T(8,128)(2,1)}, u32[]{:S(2)}, u32[]{:S(2)}) async-start(bf16[32,16,512]{2,1,0:T(8,128)(2,1)} %bitcast.48), calls=%async_computation.7 | async-start | bytes 1048576 | tf_op jit(solution)/shard_map/all_to_all | solution.py:156
  222.6 1.9 copy-done.34
  225.4 1.9 copy-done.49
  228.2 8.8 %bulk.14 = (bf16[2,1536,512]{2,1,0:T(8,128)(2,1)S(1)}, f32[2,32,512]{2,1,0:T(8,128)}) custom-call(s32[97]{0:T(128)S(1)} %pad_add_fusion.refs_0_, bf16[2,1536,512]{2,1,0:T(8,128)(2,1)S(1)} %copy-done.49, bf16[512,512]{1,0:T(8,128)(2,1)} %bitcast.23.refs_2_, bf16[2,12,4,128,128]{4,3,2,1,0:T(8,128)(2,1)S(1)} %copy-done.34, bf16[2,1536,512]{2,1,0:T(8,128)(2,1)S(1)} %copy-done.1, ...), custom_call_target="tpu_custom_call" | custom-call | flops 7000000000 | bytes 16000000 | tf_op jit(solution)/shard_map/bulk/pallas_call | solution.py:191
  237.0 1.7 copy-done.58
  239.7 1.9 copy-done.35
  241.6 1.9 copy-done.59
  243.5 9.1 %bulk.15 = (bf16[2,1536,512]{2,1,0:T(8,128)(2,1)}, f32[2,32,512]{2,1,0:T(8,128)}) custom-call(s32[97]{0:T(128)S(1)} %pad_add_fusion.refs_0_, bf16[2,1536,512]{2,1,0:T(8,128)(2,1)S(1)} %copy-done.59, bf16[512,512]{1,0:T(8,128)(2,1)} %bitcast.26.refs_2_, bf16[2,12,4,128,128]{4,3,2,1,0:T(8,128)(2,1)S(1)} %copy-done.35, bf16[2,1536,512]{2,1,0:T(8,128)(2,1)S(1)} %copy-done.1, ...), custom_call_target="tpu_custom_call" | custom-call | flops 7000000000 | bytes 16000000 | tf_op jit(solution)/shard_map/bulk/pallas_call | solution.py:191
  (149 shorter events, 53.5 us)
Async XLA Ops:
  0.0 22.9 %copy-start.69 = (s32[2,12,4]{1,2,0:T(4,128)S(1)}, s32[2,12,4]{1,2,0:T(4,128)}, u32[]{:S(2)}) copy-start(s32[2,12,4]{1,2,0:T(4,128)} %param.10) | copy-start | bytes 1156
  2.3 68.4 %collective-permute-start.5 = (bf16[512,512]{1,0:T(8,128)(2,1)}, bf16[512,512]{1,0:T(8,128)(2,1)}, u32[]{:S(2)}, u32[]{:S(2)}) collective-permute-start(bf16[512,512]{1,0:T(8,128)(2,1)} %get-tuple-element.51), channel_id=1, source_target_pairs={{0,32},{32,64},{64,96},{96,0},{1,33},{33,65},{65,97},{97,1},{2,34}... | collective-permute-start | bytes 1572872 | tf_op jit(solution)/shard_map/ppermute | solution.py:134
  2.5 68.2 %collective-permute-start.4 = (bf16[512,512]{1,0:T(8,128)(2,1)}, bf16[512,512]{1,0:T(8,128)(2,1)}, u32[]{:S(2)}, u32[]{:S(2)}) collective-permute-start(bf16[512,512]{1,0:T(8,128)(2,1)} %get-tuple-element.51), channel_id=1, source_target_pairs={{0,64},{32,96},{64,0},{96,32},{1,65},{33,97},{65,1},{97,33},{2,66}... | collective-permute-start | bytes 1572872 | tf_op jit(solution)/shard_map/ppermute | solution.py:134
  4.6 33.3 %collective-permute-start.2 = (bf16[512,512]{1,0:T(8,128)(2,1)}, bf16[512,512]{1,0:T(8,128)(2,1)}, u32[]{:S(2)}, u32[]{:S(2)}) collective-permute-start(bf16[512,512]{1,0:T(8,128)(2,1)} %get-tuple-element.52), channel_id=1, source_target_pairs={{0,32},{32,64},{64,96},{96,0},{1,33},{33,65},{65,97},{97,1},{2,34}... | collective-permute-start | bytes 1572872 | tf_op jit(solution)/shard_map/ppermute | solution.py:134
  6.1 32.3 %collective-permute-start.1 = (bf16[512,512]{1,0:T(8,128)(2,1)}, bf16[512,512]{1,0:T(8,128)(2,1)}, u32[]{:S(2)}, u32[]{:S(2)}) collective-permute-start(bf16[512,512]{1,0:T(8,128)(2,1)} %get-tuple-element.52), channel_id=1, source_target_pairs={{0,64},{32,96},{64,0},{96,32},{1,65},{33,97},{65,1},{97,33},{2,66}... | collective-permute-start | bytes 1572872 | tf_op jit(solution)/shard_map/ppermute | solution.py:134
  6.1 34.5 %collective-permute-start = (bf16[512,512]{1,0:T(8,128)(2,1)}, bf16[512,512]{1,0:T(8,128)(2,1)}, u32[]{:S(2)}, u32[]{:S(2)}) collective-permute-start(bf16[512,512]{1,0:T(8,128)(2,1)} %get-tuple-element.52), channel_id=1, source_target_pairs={{0,96},{32,0},{64,32},{96,64},{1,97},{33,1},{65,33},{97,65},{2,98}... | collective-permute-start | bytes 1572872 | tf_op jit(solution)/shard_map/ppermute | solution.py:134
  8.6 1.9 copy-start
  10.5 12.6 %copy-start.1 = (bf16[2,1536,512]{2,1,0:T(8,128)(2,1)S(1)}, bf16[2,1536,512]{2,1,0:T(8,128)(2,1)}, u32[]{:S(2)}) copy-start(bf16[2,1536,512]{2,1,0:T(8,128)(2,1)} %refs_4_.15) | copy-start | bytes 9437188
  12.9 30.7 %all-to-all-start = ((bf16[32,16,512]{2,1,0:T(8,128)(2,1)}), bf16[32,16,512]{2,1,0:T(8,128)(2,1)}, u32[]{:S(2)}, u32[]{:S(2)}) async-start(bf16[32,16,512]{2,1,0:T(8,128)(2,1)} %bitcast.54), calls=%async_computation | async-start | bytes 1048576 | tf_op jit(solution)/shard_map/all_to_all | solution.py:156
  23.1 1.9 copy-start.27
  29.6 14.0 %copy-start.26 = (f32[64,512]{1,0:T(8,128)S(1)}, f32[64,512]{1,0:T(8,128)}, u32[]{:S(2)}) copy-start(f32[64,512]{1,0:T(8,128)} %copy-done.25) | copy-start | bytes 393220
  37.9 32.8 %collective-permute-start.3 = (bf16[512,512]{1,0:T(8,128)(2,1)}, bf16[512,512]{1,0:T(8,128)(2,1)}, u32[]{:S(2)}, u32[]{:S(2)}) collective-permute-start(bf16[512,512]{1,0:T(8,128)(2,1)} %get-tuple-element.51), channel_id=1, source_target_pairs={{0,96},{32,0},{64,32},{96,64},{1,97},{33,1},{65,33},{97,65},{2,98}... | collective-permute-start | bytes 1572872 | tf_op jit(solution)/shard_map/ppermute | solution.py:134
  47.1 26.4 %all-to-all-start.1 = ((bf16[32,16,512]{2,1,0:T(8,128)(2,1)}), bf16[32,16,512]{2,1,0:T(8,128)(2,1)}, u32[]{:S(2)}, u32[]{:S(2)}) async-start(bf16[32,16,512]{2,1,0:T(8,128)(2,1)} %bitcast.47), calls=%async_computation.1 | async-start | bytes 1048576 | tf_op jit(solution)/shard_map/all_to_all | solution.py:156
  57.2 1.9 copy-start.28
  60.9 9.8 %copy-start.68 = (bf16[2,512,512]{2,1,0:T(8,128)(2,1)S(1)}, bf16[2,512,512]{2,1,0:T(8,128)(2,1)}, u32[]{:S(2)}) copy-start(bf16[2,512,512]{2,1,0:T(8,128)(2,1)} %param.8) | copy-start | bytes 3145732
  69.0 1.7 copy-start.46
  77.1 23.9 %all-to-all-start.2 = ((bf16[32,16,512]{2,1,0:T(8,128)(2,1)}), bf16[32,16,512]{2,1,0:T(8,128)(2,1)}, u32[]{:S(2)}, u32[]{:S(2)}) async-start(bf16[32,16,512]{2,1,0:T(8,128)(2,1)} %bitcast.49), calls=%async_computation.2 | async-start | bytes 1048576 | tf_op jit(solution)/shard_map/all_to_all | solution.py:156
  84.5 1.0 copy-start.13
  85.6 1.9 copy-start.29
  88.4 1.9 copy-start.47
  99.3 1.7 copy-start.50
  101.0 1.0 copy-start.8
  104.5 23.9 %all-to-all-start.3 = ((bf16[32,16,512]{2,1,0:T(8,128)(2,1)}), bf16[32,16,512]{2,1,0:T(8,128)(2,1)}, u32[]{:S(2)}, u32[]{:S(2)}) async-start(bf16[32,16,512]{2,1,0:T(8,128)(2,1)} %bitcast.50), calls=%async_computation.3 | async-start | bytes 1048576 | tf_op jit(solution)/shard_map/all_to_all | solution.py:156
  113.0 1.9 copy-start.30
  115.8 1.9 copy-start.51
  126.7 1.7 copy-start.52
  128.4 1.0 copy-start.10
  131.9 23.9 %all-to-all-start.4 = ((bf16[32,16,512]{2,1,0:T(8,128)(2,1)}), bf16[32,16,512]{2,1,0:T(8,128)(2,1)}, u32[]{:S(2)}, u32[]{:S(2)}) async-start(bf16[32,16,512]{2,1,0:T(8,128)(2,1)} %bitcast.51), calls=%async_computation.4 | async-start | bytes 1048576 | tf_op jit(solution)/shard_map/all_to_all | solution.py:156
  139.3 1.0 copy-start.11
  140.4 1.9 copy-start.31
  143.2 1.9 copy-start.53
  154.1 1.7 copy-start.54
  159.3 23.9 %all-to-all-start.5 = ((bf16[32,16,512]{2,1,0:T(8,128)(2,1)}), bf16[32,16,512]{2,1,0:T(8,128)(2,1)}, u32[]{:S(2)}, u32[]{:S(2)}) async-start(bf16[32,16,512]{2,1,0:T(8,128)(2,1)} %bitcast.52), calls=%async_computation.5 | async-start | bytes 1048576 | tf_op jit(solution)/shard_map/all_to_all | solution.py:156
  167.8 1.9 copy-start.32
  170.6 1.9 copy-start.55
  181.5 1.7 copy-start.56
  186.7 23.9 %all-to-all-start.6 = ((bf16[32,16,512]{2,1,0:T(8,128)(2,1)}), bf16[32,16,512]{2,1,0:T(8,128)(2,1)}, u32[]{:S(2)}, u32[]{:S(2)}) async-start(bf16[32,16,512]{2,1,0:T(8,128)(2,1)} %bitcast.53), calls=%async_computation.6 | async-start | bytes 1048576 | tf_op jit(solution)/shard_map/all_to_all | solution.py:156
  195.2 1.9 copy-start.33
  198.0 1.9 copy-start.57
  209.0 1.7 copy-start.48
  214.1 24.6 %all-to-all-start.7 = ((bf16[32,16,512]{2,1,0:T(8,128)(2,1)}), bf16[32,16,512]{2,1,0:T(8,128)(2,1)}, u32[]{:S(2)}, u32[]{:S(2)}) async-start(bf16[32,16,512]{2,1,0:T(8,128)(2,1)} %bitcast.48), calls=%async_computation.7 | async-start | bytes 1048576 | tf_op jit(solution)/shard_map/all_to_all | solution.py:156
  222.6 1.9 copy-start.34
  225.4 1.9 copy-start.49
  228.2 10.5 %copy-start.45 = (f32[64,512]{1,0:T(8,128)S(1)}, f32[64,512]{1,0:T(8,128)}, u32[]{:S(2)}) copy-start(f32[64,512]{1,0:T(8,128)} %copy-done.36) | copy-start | bytes 393220
  237.0 1.7 copy-start.58
  238.7 1.0 copy-start.23
  239.7 1.9 copy-start.35
  241.6 1.9 copy-start.59
  (36 other events, 32.5 us)
